TPU v7x, 512 devices: a whole 4x4x16 slice. The times are simulated.
512 devices in a mesh: fsdp: 64 (over z, x), tensor: 8 (over y, core).
Axes of the slice: x: 4, y: 4, z: 16, core: 2. Of those that a mesh axis runs over, the one named last changes fastest.
Arguments:
- momentum: float32 [8192, 26624], P('fsdp', 'tensor'), may hold values from -64 to 64
- gradient: bfloat16 [8192, 26624], P('fsdp', 'tensor'), may hold values from -6 to 6
- basis: float32 [256, 26624], P('fsdp', 'tensor'), may hold values from -0.0390625 to 0.0390625
Outputs:
- new_momentum: float32 [8192, 26624], P('fsdp', 'tensor')
- weight_delta: bfloat16 [8192, 26624], P('fsdp', 'tensor')
All inputs are finite; a program needn't handle non-finite values.
Results may differ from a plain program's by a relative error of at most 0.003.
Values sent between devices are 32-bit elements; how exact they have to be, the bound alone decides.
A program may use at most 64 MiB of HBM per device.

v0:
```python
import jax
import jax.numpy as jnp
from jax import lax
from jax.sharding import PartitionSpec as P

ROWS = 8192
COLS = 26624
RANK = 256


def gram_of(rows_block):
    return jnp.dot(
        rows_block.T,
        rows_block,
        precision=lax.Precision.HIGHEST,
        preferred_element_type=jnp.float32,
    )


def orthonormal(rows_block, gram):
    lower = jnp.linalg.cholesky(gram)
    return jax.scipy.linalg.solve_triangular(lower, rows_block.T, lower=True).T


def per_device(momentum, gradient, basis):
    high = lax.Precision.HIGHEST
    blend = momentum + gradient.astype(jnp.float32)
    partial_proj = lax.dot_general(
        blend,
        lax.all_gather(basis, "fsdp", axis=0, tiled=True),
        (((1,), (1,)), ((), ())),
        precision=high,
        preferred_element_type=jnp.float32,
    )
    proj = lax.psum(partial_proj, "tensor")
    gram = lax.psum(gram_of(proj), "fsdp")
    ortho = orthonormal(proj, gram)
    partial_right = lax.dot_general(
        ortho, blend, (((0,), (0,)), ((), ())), precision=high, preferred_element_type=jnp.float32
    )
    right = lax.psum(partial_right, "fsdp")
    squared = lax.psum(jnp.sum(right * right, axis=1), "tensor")
    inverse = 1.0 / (jnp.sqrt(squared) + 1e-06)
    feedback = jnp.dot(ortho, right, precision=high, preferred_element_type=jnp.float32)
    update = jnp.dot(
        ortho, right * inverse[:, None], precision=high, preferred_element_type=jnp.float32
    )
    new_momentum = blend - 0.05 * feedback
    factor = (ROWS * COLS / RANK) ** 0.5
    weight_delta = (-factor * update).astype(jnp.bfloat16)
    return (new_momentum, weight_delta)


def solution(mesh):
    in_specs = (P("fsdp", "tensor"), P("fsdp", "tensor"), P("fsdp", "tensor"))
    out_specs = (P("fsdp", "tensor"), P("fsdp", "tensor"))
    return jax.shard_map(
        per_device, mesh=mesh, in_specs=in_specs, out_specs=out_specs, check_vma=False
    )
```

profile of v0, /device:TPU:1, one launch (start us, length us, event | category | flops | bytes accessed | tf_op | source)
XLA Modules:
  0.0 886.4 jit_solution(10506621002460734175)
XLA Ops:
  7.2 0.7 all-gather.3.cloned.1.call-update
  8.0 144.7 %all-gather.3.cloned.1.call-done = f32[64,4,3328]{2,1,0:T(4,128)} async-done(((f32[1,4,3328]{2,1,0:T(4,128)}), f32[64,4,3328]{2,1,0:T(4,128)}) %all-gather.3.cloned.1.call-update) | async-done | bytes 3407888 | tf_op jit(solution)/shard_map/all_gather | solution.py:30
  152.6 5.1 reshape.44
  157.7 6.1 fusion.5
  163.9 76.4 %all-reduce.5.cloned.1.call-done = f32[128,256]{1,0:T(8,128)} async-done(((f32[128,256]{1,0:T(8,128)}), f32[128,256]{1,0:T(8,128)}) %all-reduce.5.cloned.1.call-update) | async-done | bytes 131088 | tf_op jit(solution)/shard_map/psum | solution.py:35
  240.3 2.1 fusion.18
  242.6 255.3 %all-reduce.7.cloned.1.call-done = f32[256,256]{0,1:T(8,128)} async-done(((f32[256,256]{0,1:T(8,128)}), f32[256,256]{0,1:T(8,128)}) %all-reduce.7.cloned.1.call-update) | async-done | bytes 262160 | tf_op jit(solution)/shard_map/psum | solution.py:36
  498.0 1.1 copy.8
  499.1 1.0 fusion.6
  500.1 11.7 %cholesky.50 = f32[128,128]{1,0:T(8,128)S(1)} custom-call(f32[128,128]{1,0:T(8,128)S(1)} %cholesky.118), custom_call_target="Cholesky" | custom-call | tf_op jit(solution)/shard_map/jit(cholesky)/cholesky | solution.py:21
  511.8 9.8 %custom-call.15 = f32[1,128,128]{1,2,0:T(8,128)S(1)} custom-call(f32[1,128,128]{2,1,0:T(8,128)S(1)} %get-tuple-element.23), custom_call_target="InvertDiagBlocksLowerTriangular" | custom-call | tf_op jit(solution)/shard_map/jit(cholesky)/cholesky | solution.py:21
  522.2 11.7 %cholesky.105 = f32[128,128]{1,0:T(8,128)S(1)} custom-call(f32[128,128]{1,0:T(8,128)S(1)} %convolution_subtract_fusion.1), custom_call_target="Cholesky" | custom-call | tf_op jit(solution)/shard_map/jit(cholesky)/cholesky | solution.py:21
  533.9 0.7 compare_reduce_fusion
  536.1 5.5 while.1
  536.9 2.1 bitcast_dynamic-update-slice_fusion.2
  539.0 0.6 fusion.28
  539.5 2.1 bitcast_dynamic-update-slice_fusion.2
  541.6 20.5 %custom-call.16 = f32[2,128,128]{1,2,0:T(8,128)S(1)} custom-call(f32[2,128,128]{2,1,0:T(8,128)} %get-tuple-element.9), custom_call_target="InvertDiagBlocksLowerTriangular" | custom-call | tf_op jit(solution)/shard_map/jit(_solve_triangular)/triangular_solve | solution.py:22
  563.0 4.6 fusion.4
  567.6 280.9 %all-reduce.9.cloned.1.call-done = f32[256,3328]{1,0:T(8,128)} async-done(((f32[256,3328]{1,0:T(8,128)}), f32[256,3328]{1,0:T(8,128)}) %all-reduce.9.cloned.1.call-update) | async-done | bytes 3407888 | tf_op jit(solution)/shard_map/psum | solution.py:41
  848.5 2.4 multiply_reduce_fusion
  850.9 21.0 %psum.31 = f32[256]{0:T(256)S(1)} all-reduce(f32[256]{0:T(256)S(1)} %multiply_reduce_fusion), channel_id=1, replica_groups=mesh['fsdp'=64,'tensor'=8] {'tensor'}, use_global_device_ids=true, to_apply=%region_8.9 | all-reduce | flops 256 | bytes 2048 | tf_op jit(solution)/shard_map/psum | solution.py:42
  871.9 4.9 fusion
  876.8 3.1 fusion.1
  (32 shorter events, 2.6 us)
Async XLA Ops:
  7.2 145.5 %all-gather.3.cloned.1.call-start = ((), (), s32[]{:S(2)}) async-start(), calls=%async_computation.3 | async-start | bytes 3461120 | tf_op jit(solution)/shard_map/all_gather | solution.py:30
  7.9 149.8 %copy-start.1 = (f32[128,3328]{1,0:T(8,128)S(1)}, f32[128,3328]{1,0:T(8,128)}, u32[]{:S(2)}) copy-start(f32[128,3328]{1,0:T(8,128)} %param.3) | copy-start | bytes 5111812
  7.9 149.8 %copy-start.2 = (bf16[128,3328]{1,0:T(8,128)(2,1)S(1)}, bf16[128,3328]{1,0:T(8,128)(2,1)}, u32[]{:S(2)}) copy-start(bf16[128,3328]{1,0:T(8,128)(2,1)} %param.4) | copy-start | bytes 2555908
  7.9 232.3 %all-reduce.5.cloned.1.call-start = ((), (), s32[]{:S(2)}) async-start(), calls=%async_computation | async-start | bytes 262144 | tf_op jit(solution)/shard_map/psum | solution.py:35
  163.8 334.2 %all-reduce.7.cloned.1.call-start = ((), (), s32[]{:S(2)}) async-start(), calls=%async_computation.1 | async-start | bytes 524288 | tf_op jit(solution)/shard_map/psum | solution.py:36
  242.4 606.1 %all-reduce.9.cloned.1.call-start = ((), (), s32[]{:S(2)}) async-start(), calls=%async_computation.2 | async-start | bytes 6815744 | tf_op jit(solution)/shard_map/psum | solution.py:41
  499.1 63.0 %copy-start.3 = (f32[128,256]{1,0:T(8,128)S(1)}, f32[128,256]{1,0:T(8,128)}, u32[]{:S(2)}) copy-start(f32[128,256]{1,0:T(8,128)} %all-reduce.5.cloned.1.call-done) | copy-start | bytes 393220
  848.5 23.4 %copy-start = (f32[256,3328]{1,0:T(8,128)S(1)}, f32[256,3328]{1,0:T(8,128)}, u32[]{:S(2)}) copy-start(f32[256,3328]{1,0:T(8,128)} %all-reduce.9.cloned.1.call-done) | copy-start | bytes 10223620
Sparse Core Ops, SparseCore 0:
  11.0 141.6 all-gather.2
  163.9 76.2 all-reduce.4
  244.7 253.2 all-reduce.6
  567.7 280.6 all-reduce.8
where the time goes:
time: 887 us; the launch traced here: 886 us
  waiting for transfers between devices  758 us (85%)
  other arithmetic  58 us (7%)
  matrix products  22.1 us (2%)
  blocking collectives  21 us (2%)
  between operations  15.2 us (2%)
  local copies, waits for them, and re-layouts  11.6 us (1%)
    psum x1, waiting for transfers between devices, per_device(): right = lax.psum(partial_right, 'fsdp')  281 us
    psum x1, waiting for transfers between devices, per_device(): gram = lax.psum(gram_of(proj), 'fsdp')  255 us
    all_gather x1, waiting for transfers between devices, per_device(): lax.all_gather(basis, 'fsdp', axis=0, tiled=True)  145 us
    psum x1, waiting for transfers between devices, per_device(): proj = lax.psum(partial_proj, 'tensor')  76.4 us
    another operation x6, other arithmetic, orthonormal(): lower = jnp.linalg.cholesky(gram)  34 us
    psum x1, blocking collectives, per_device(): squared = lax.psum(jnp.sum(right * right, axis=1), 'tensor')  21 us
    another operation x3, other arithmetic, orthonormal(): return jax.scipy.linalg.solve_triangular(lower, rows_block.T, lower=True).T  20.5 us
  transfers between devices with their start and end apart: 4, of which 4 were waited for; matrix products, arithmetic and copies ran while one was open for 0% of the time, Pallas kernels for 0%

commit v1 on v0

v1 whole, which is shorter than its diff:
```python
import functools

import jax
import jax.numpy as jnp
from jax import lax
from jax.experimental import pallas as pl
from jax.experimental.pallas import tpu as pltpu
from jax.sharding import PartitionSpec as P

ROWS = 8192
COLS = 26624
RANK = 256
NX = 4
GROUPS = RANK // 4
PANEL = 32
F32 = jnp.float32
BF16 = jnp.bfloat16
HIGHEST = lax.Precision.HIGHEST
NT = (((1,), (1,)), ((), ()))
TN = (((0,), (0,)), ((), ()))
NN = (((1,), (0,)), ((), ()))


def split(value):
    high = value.astype(BF16)
    return high, (value - high.astype(F32)).astype(BF16)


def dot(a, b, dims):
    return lax.dot_general(a, b, dims, preferred_element_type=F32)


def dot3(a, b, dims):
    (ah, al), (bh, bl) = a, b
    return dot(ah, bh, dims) + (dot(ah, bl, dims) + dot(al, bh, dims))


def dot_full(a, b, dims):
    return lax.dot_general(a, b, dims, precision=HIGHEST, preferred_element_type=F32)


def kernel(
    nz, nt, factor,
    mom_hbm, grad_hbm, basis_hbm, newm_hbm, delta_hbm,
    mom, grad, bhi, blo, vbuf, part, proj, rsbuf,
    wbuf, ropp, rleft, rright, rz, wfin,
    gram, gslice, grs, gsum, gx, gall, elim,
    rhi, rlo, nbuf, dout,
    load_sem, store_sem, v_send, v_z, v_l, v_r, v_o,
    w_send, w_z, w_l, w_r, w_o, r_send, r_z, r_l, r_r, r_o,
    s_send, s_recv,
):
    rows, cols = mom.shape
    nblk = cols // 128
    nh = nblk // 2
    half = nz // 2
    m = GROUPS // (nz * NX)
    f = lax.axis_index("fsdp")
    t = lax.axis_index("tensor")
    z, x = lax.div(f, NX), lax.rem(f, NX)
    left, right, opp = lax.rem(x + NX - 1, NX), lax.rem(x + 1, NX), lax.rem(x + 2, NX)

    def zmod(value):
        return lax.rem(value + nz, nz)

    def tmod(value):
        return lax.rem(value + nt, nt)

    def dev(zz, xx):
        return (zz * NX + xx, t)

    to_up, to_down = dev(zmod(z + 1), x), dev(zmod(z - 1), x)
    to_left, to_right, to_opp = dev(z, left), dev(z, right), dev(z, opp)

    def remote(src, dst, send, recv, device):
        return pltpu.make_async_remote_copy(
            src_ref=src, dst_ref=dst, send_sem=send, recv_sem=recv,
            device_id=device, device_id_type=pl.DeviceIdType.MESH,
        )

    def wait(ref, sem):
        pltpu.make_async_copy(ref, ref, sem).wait()

    load_basis = pltpu.make_async_copy(basis_hbm, vbuf.at[pl.ds(f * m, m)], load_sem.at[0])
    load_mom = pltpu.make_async_copy(mom_hbm, mom, load_sem.at[1])
    load_grad = pltpu.make_async_copy(grad_hbm, grad, load_sem.at[2])
    load_basis.start()
    load_mom.start()
    load_grad.start()

    barrier = pltpu.get_barrier_semaphore()

    def greet(device):
        pl.semaphore_signal(barrier, inc=1, device_id=device, device_id_type=pl.DeviceIdType.MESH)

    def greet_z(r, carry):
        greet(dev(zmod(z + r), x))
        return carry

    def greet_t(r, carry):
        greet((f, tmod(t + r)))
        return carry

    lax.fori_loop(1, nz, greet_z, 0)
    lax.fori_loop(1, nt, greet_t, 0)
    for device in (to_left, to_right, to_opp):
        greet(device)
    pl.semaphore_wait(barrier, (nz - 1) + (nt - 1) + 3)

    def gather(buf, send, sz, sl, sr, so, early, hook):
        def at(zz, xx):
            return buf.at[pl.ds((zz * NX + xx) * m, m)]

        def push(zz, xx, sem, device):
            remote(at(zz, xx), at(zz, xx), send, sem.at[zz], device).start()

        def spread(zz):
            push(zz, x, sl, to_right)
            push(zz, x, sr, to_left)

        def pass_right(zz):
            wait(at(zz, left), sl.at[zz])
            push(zz, left, so, to_right)

        def pass_left(zz):
            wait(at(zz, right), sr.at[zz])
            push(zz, right, so, to_left)

        push(z, x, sz, to_up)
        if half > 1:
            push(z, x, sz, to_down)
        spread(z)
        early()

        def step(j, carry):
            below, above = zmod(z - j), zmod(z + j)
            wait(at(below, x), sz.at[below])

            @pl.when(j < half)
            def _():
                push(below, x, sz, to_up)

            spread(below)

            @pl.when(j < half)
            def _():
                wait(at(above, x), sz.at[above])

                @pl.when(j < half - 1)
                def _():
                    push(above, x, sz, to_down)

                spread(above)

            pass_right(zmod(z - j + 1))

            @pl.when(j > 1)
            def _():
                pass_left(zmod(z + j - 1))

            hook(j)
            return carry

        lax.fori_loop(1, half + 1, step, 0)
        pass_right(zmod(z - half))

        def finish(j, carry):
            below, above = zmod(z - j), zmod(z + j)
            wait(at(below, right), sr.at[below])
            wait(at(below, opp), so.at[below])

            @pl.when((j > 0) & (j < half))
            def _():
                wait(at(above, left), sl.at[above])
                wait(at(above, opp), so.at[above])

            return carry

        lax.fori_loop(0, half + 1, finish, 0)
        wait(buf.at[pl.ds(0, (nz * NX - 1) * m)], send)

    load_basis.wait()

    def make_blend():
        load_mom.wait()
        load_grad.wait()

        def body(c, carry):
            cut = pl.ds(pl.multiple_of(c * 256, 256), 256)
            blend = mom[:, cut] + grad[:, cut].astype(F32)
            mom[:, cut] = blend
            bhi[:, cut], blo[:, cut] = split(blend)
            return carry

        lax.fori_loop(0, nblk // 2, body, 0)

    gather(vbuf, v_send.at[0], v_z, v_l, v_r, v_o, make_blend, lambda j: None)

    def project(c, acc):
        cut = pl.ds(pl.multiple_of(c * 256, 256), 256)
        pair = [vbuf[:, 2 * c + k].reshape(RANK, 128) for k in range(2)]
        return acc + dot3((bhi[:, cut], blo[:, cut]), split(jnp.concatenate(pair, axis=1)), NT)

    part[...] = lax.fori_loop(0, nblk // 2, project, jnp.zeros((rows, RANK), F32))

    share = rows // nt
    if nt > 1:
        own = pl.ds(t * share, share)

        def send_part(r, carry):
            peer = tmod(t + r)
            remote(
                part.at[pl.ds(peer * share, share)], rsbuf.at[r - 1],
                s_send.at[0], s_recv.at[0], (f, peer),
            ).start()
            return carry

        lax.fori_loop(1, nt, send_part, 0)
        wait(rsbuf, s_recv.at[0])
        total = part[own]
        for r in range(nt - 1):
            total = total + rsbuf[r]
        proj[own] = total

        def send_sum(r, carry):
            remote(
                proj.at[own], proj.at[own], s_send.at[1], s_recv.at[1], (f, tmod(t + r))
            ).start()
            return carry

        lax.fori_loop(1, nt, send_sum, 0)
        wait(proj.at[pl.ds(0, (nt - 1) * share)], s_recv.at[1])
        wait(rsbuf, s_send.at[0])
        wait(proj.at[pl.ds(0, (nt - 1) * share)], s_send.at[1])
    else:
        proj[...] = part[...]

    full = proj[...]
    gram[...] = dot_full(full, full, TN)
    gshare = RANK // nt
    ng = 2 * gshare // 4
    mg = ng // nz
    mine = gram[pl.ds(t * gshare, gshare), :]
    for r in range(gshare // 4):
        for c in range(2):
            gslice[2 * r + c] = mine[4 * r : 4 * r + 4, 128 * c : 128 * c + 128]

    def gram_send():
        def body(r, carry):
            peer = zmod(z + r)
            remote(
                gslice.at[pl.ds(peer * mg, mg)], grs.at[r - 1],
                s_send.at[2], s_recv.at[2], dev(peer, x),
            ).start()
            return carry

        lax.fori_loop(1, nz, body, 0)

    def gram_over_z():
        wait(grs, s_recv.at[2])
        gsum[...] = gslice[pl.ds(z * mg, mg)] + jnp.sum(grs[...], axis=0)
        gx[x] = gsum[...]
        for k, device in enumerate((to_left, to_right, to_opp)):
            remote(gsum, gx.at[x], s_send.at[3], s_recv.at[3], device).start()

    def gram_over_x():
        wait(gx.at[pl.ds(0, NX - 1)], s_recv.at[3])
        here = pl.ds(t * ng + z * mg, mg)
        gall[here] = jnp.sum(gx[...], axis=0)

        def body(r, carry):
            remote(
                gall.at[here], gall.at[here], s_send.at[4], s_recv.at[4], dev(zmod(z + r), x)
            ).start()
            return carry

        lax.fori_loop(1, nz, body, 0)

    def gram_over_t():
        wait(gall.at[pl.ds(0, (nz - 1) * mg)], s_recv.at[4])
        if nt > 1:
            here = pl.ds(t * ng, ng)

            def body(r, carry):
                remote(
                    gall.at[here], gall.at[here], s_send.at[5], s_recv.at[5], (f, tmod(t + r))
                ).start()
                return carry

            lax.fori_loop(1, nt, body, 0)

    def gram_done():
        if nt > 1:
            wait(gall.at[pl.ds(0, (nt - 1) * ng)], s_recv.at[5])
            wait(gall.at[pl.ds(0, (nt - 1) * ng)], s_send.at[5])
        wait(grs, s_send.at[2])
        wait(gx.at[pl.ds(0, NX - 1)], s_send.at[3])
        wait(gall.at[pl.ds(0, (nz - 1) * mg)], s_send.at[4])
        for r in range(RANK // 8):
            for c in range(2):
                pair = [gall[4 * r + c], gall[4 * r + 2 + c]]
                elim[8 * r : 8 * r + 8, 128 * c : 128 * c + 128] = jnp.concatenate(pair, axis=0)
        down = lax.broadcasted_iota(jnp.int32, (RANK, RANK), 0)
        across = lax.broadcasted_iota(jnp.int32, (RANK, RANK), 1)
        elim[:, RANK:] = jnp.where(down == across, 1.0, 0.0).astype(F32)

    gram_send()

    turned = split(full.T)
    for h in range(2):
        start = 0
        while start < nh:
            width = min(4, nh - start) if nh - start != 5 else 5
            cut = slice((h * nh + start) * 128, (h * nh + start + width) * 128)
            out = dot3(turned, (bhi[:, cut], blo[:, cut]), NN)
            for k in range(width):
                for r in range(RANK // 8):
                    wbuf[2 * r + h, start + k] = out[8 * r : 8 * r + 8, 128 * k : 128 * k + 128]
            start += width

    def piece(buf, index):
        return buf.at[pl.ds(index * m, m)]

    def wat(q, xx):
        return piece(wbuf, q * NX + xx)

    def add_into(ref, other):
        ref[...] = ref[...] + other[...]

    def stage_a(q, s):
        remote(wat(q, opp), piece(ropp, q), r_send.at[0], r_o.at[q], (to_right, to_left)[s]).start()

    def stage_b(q, s):
        wait(piece(ropp, q), r_o.at[q])
        add_into(wat(q, (right, left)[s]), piece(ropp, q))
        remote(wat(q, right), piece(rleft, q), r_send.at[0], r_l.at[q], to_right).start()
        remote(wat(q, left), piece(rright, q), r_send.at[0], r_r.at[q], to_left).start()

    def stage_c(q):
        wait(piece(rleft, q), r_l.at[q])
        wait(piece(rright, q), r_r.at[q])
        here = wat(q, x)
        here[...] = here[...] + (piece(rleft, q)[...] + piece(rright, q)[...])

    def stage_z(q, slot, device):
        remote(wat(q, x), piece(rz, slot), r_send.at[0], r_z.at[slot], device).start()

    def take_z(q, slot):
        wait(piece(rz, slot), r_z.at[slot])
        add_into(wat(q, x), piece(rz, slot))

    def reduce_step(i, carry):
        @pl.when(i <= half)
        def _():
            stage_a(zmod(z - half + i), 0)

        @pl.when((i >= 1) & (i < half))
        def _():
            stage_a(zmod(z + half - i), 1)

        b = i - 1

        @pl.when((b >= 0) & (b <= half))
        def _():
            stage_b(zmod(z - half + b), 0)

        @pl.when((b >= 1) & (b < half))
        def _():
            stage_b(zmod(z + half - b), 1)

        c = i - 2

        @pl.when(c >= 0)
        def _():
            q = zmod(z - half + c)
            stage_c(q)

            @pl.when(c > 0)
            def _():
                take_z(q, q)

            @pl.when(c < half)
            def _():
                stage_z(q, q, to_down)

        @pl.when((c >= 1) & (c < half))
        def _():
            q = zmod(z + half - c)
            stage_c(q)

            @pl.when(c > 1)
            def _():
                take_z(q, q)

            stage_z(q, lax.select(c == half - 1, nz, q), to_up)

        if half > 1:
            @pl.when(c == half)
            def _():
                take_z(z, nz)

        @pl.when(i == max(1, half // 4))
        def _():
            gram_over_z()

        @pl.when(i == max(2, half // 2))
        def _():
            gram_over_x()

        @pl.when(i == max(3, 3 * half // 4))
        def _():
            gram_over_t()

        return carry

    lax.fori_loop(0, half + 3, reduce_step, 0)
    piece(wfin, f)[...] = wat(z, x)[...]
    gram_done()

    lane = lax.broadcasted_iota(jnp.int32, (PANEL, 128), 1)
    down = lax.broadcasted_iota(jnp.int32, (PANEL, 128), 0)
    wide = lax.broadcasted_iota(jnp.int32, (PANEL, RANK), 1)
    npanel = RANK // PANEL

    def panel(b):
        here = pl.ds(pl.multiple_of(b * PANEL, PANEL), PANEL)
        block = elim[here, :]
        turned = pltpu.roll(block[:, :RANK], lax.rem(RANK - b * PANEL, RANK), 1)[:, :128]
        state = jnp.where(lane < PANEL, turned, jnp.where(lane == down + PANEL, 1.0, 0.0))
        for j in range(PANEL - 1):
            row = state[j : j + 1, :]
            scale = state[:, j : j + 1] / state[j : j + 1, j : j + 1]
            state = state - jnp.where(down > j, scale, 0.0) * row
        diag = jnp.sum(jnp.where(lane == down, state, 0.0), axis=1, keepdims=True)
        lower = state[:, PANEL : 2 * PANEL] / jnp.sqrt(diag)
        done = dot_full(lower, block, NN)
        rest = jnp.where(wide >= (b + 1) * PANEL, done[:, :RANK], 0.0)
        elim[...] = elim[...] - dot_full(rest, done, TN)
        elim[here, :] = done

    def panels(j):
        for k in range(npanel // half):
            panel((j - 1) * (npanel // half) + k)

    gather(wfin, w_send.at[0], w_z, w_l, w_r, w_o, lambda: None, panels)
    wait(wbuf.at[pl.ds(0, (nz * NX - 1) * m)], r_send.at[0])

    inv_lower = elim[:, RANK:]
    ortho = dot_full(proj[...], inv_lower, NT)
    low = split(inv_lower)
    squared = jnp.zeros((RANK, 128), F32)
    cuts = []
    for h in range(2):
        start = 0
        while start < nh:
            width = min(4, nh - start) if nh - start != 5 else 5
            cuts.append((h, start, width))
            start += width
    for h, start, width in cuts:
        cut = slice((h * nh + start) * 128, (h * nh + start + width) * 128)
        columns = [
            jnp.concatenate([wfin[2 * r + h, start + k] for r in range(RANK // 8)], axis=0)
            for k in range(width)
        ]
        out = dot3(low, split(jnp.concatenate(columns, axis=1)), NN)
        for k in range(width):
            one = out[:, 128 * k : 128 * k + 128]
            squared = squared + one * one
        rhi[:, cut], rlo[:, cut] = split(out)
    nbuf[t] = dot_full(jnp.ones((8, 128), F32), squared, NT)

    if nt > 1:
        def send_norm(r, carry):
            remote(
                nbuf.at[t], nbuf.at[t], s_send.at[6], s_recv.at[6], (f, tmod(t + r))
            ).start()
            return carry

        lax.fori_loop(1, nt, send_norm, 0)

    ortho_high = ortho.astype(BF16)
    stores = []
    for n, (h, start, width) in enumerate(cuts):
        cut = slice((h * nh + start) * 128, (h * nh + start + width) * 128)
        mom[:, cut] = mom[:, cut] - 0.05 * dot(ortho_high, rhi[:, cut], NN)
        stores.append(pltpu.make_async_copy(mom.at[:, cut], newm_hbm.at[:, cut], store_sem.at[n]))
        stores[-1].start()

    if nt > 1:
        wait(nbuf.at[pl.ds(0, nt - 1)], s_recv.at[6])
        wait(nbuf.at[pl.ds(0, nt - 1)], s_send.at[6])
    norm = nbuf[0]
    for r in range(1, nt):
        norm = norm + nbuf[r]
    inverse = 1.0 / (jnp.sqrt(norm) + 1e-06)
    scaled = split(ortho * (inverse[0:1, :] * -factor))
    for n, (h, start, width) in enumerate(cuts):
        cut = slice((h * nh + start) * 128, (h * nh + start + width) * 128)
        dout[:, cut] = dot3(scaled, (rhi[:, cut], rlo[:, cut]), NN).astype(BF16)
        stores.append(
            pltpu.make_async_copy(dout.at[:, cut], delta_hbm.at[:, cut], store_sem.at[len(cuts) + n])
        )
        stores[-1].start()
    for store in stores:
        store.wait()


def per_device(nz, nt, factor, momentum, gradient, basis):
    rows, cols = momentum.shape
    nblk = cols // 128
    nh = nblk // 2
    m = GROUPS // (nz * NX)
    gshare = RANK // nt
    ng = 2 * gshare // 4
    mg = ng // nz
    tiles = basis.reshape(m, 4, nblk, 128).transpose(0, 2, 1, 3)
    vmem = pltpu.VMEM
    dma = pltpu.SemaphoreType.DMA
    any_spec = pl.BlockSpec(memory_space=pl.ANY)
    one = max(nt - 1, 1)
    return pl.pallas_call(
        functools.partial(kernel, nz, nt, factor),
        out_shape=(
            jax.ShapeDtypeStruct((rows, cols), F32),
            jax.ShapeDtypeStruct((rows, cols), BF16),
        ),
        in_specs=[any_spec] * 3,
        out_specs=(any_spec, any_spec),
        scratch_shapes=[
            vmem((rows, cols), F32),
            vmem((rows, cols), BF16),
            vmem((rows, cols), BF16),
            vmem((rows, cols), BF16),
            vmem((GROUPS, nblk, 4, 128), F32),
            vmem((rows, RANK), F32),
            vmem((rows, RANK), F32),
            vmem((one, rows // nt, RANK), F32),
            vmem((GROUPS, nh, 8, 128), F32),
            vmem((nz * m, nh, 8, 128), F32),
            vmem((nz * m, nh, 8, 128), F32),
            vmem((nz * m, nh, 8, 128), F32),
            vmem(((nz + 1) * m, nh, 8, 128), F32),
            vmem((GROUPS, nh, 8, 128), F32),
            vmem((RANK, RANK), F32),
            vmem((ng, 4, 128), F32),
            vmem((nz - 1, mg, 4, 128), F32),
            vmem((mg, 4, 128), F32),
            vmem((NX, mg, 4, 128), F32),
            vmem((2 * GROUPS, 4, 128), F32),
            vmem((RANK, 2 * RANK), F32),
            vmem((RANK, cols), BF16),
            vmem((RANK, cols), BF16),
            vmem((nt, 8, RANK), F32),
            vmem((rows, cols), BF16),
            dma((3,)),
            dma((16,)),
            dma((1,)), dma((nz,)), dma((nz,)), dma((nz,)), dma((nz,)),
            dma((1,)), dma((nz,)), dma((nz,)), dma((nz,)), dma((nz,)),
            dma((1,)), dma((nz + 1,)), dma((nz,)), dma((nz,)), dma((nz,)),
            dma((7,)),
            dma((7,)),
        ],
        compiler_params=pltpu.CompilerParams(
            collective_id=0, has_side_effects=True, vmem_limit_bytes=56 * 2**20
        ),
        name="dion_step",
    )(momentum, gradient, tiles)


def solution(mesh):
    nz, nt = mesh.shape["fsdp"] // NX, mesh.shape["tensor"]
    factor = (ROWS * COLS / RANK) ** 0.5
    spec = P("fsdp", "tensor")
    return jax.shard_map(
        functools.partial(per_device, nz, nt, factor),
        mesh=mesh, in_specs=(spec,) * 3, out_specs=(spec,) * 2, check_vma=False,
    )
```

time: 887 us -> 156 us (0.18)
  waiting for transfers between devices: 758 us -> 0 us
  Pallas kernels: 0 us -> 151 us
  other arithmetic: 58 us -> 0 us
  matrix products: 22.1 us -> 0 us
  blocking collectives: 21 us -> 0 us
  between operations: 15.2 us -> 0.65 us
    psum x3 -> x0, waiting for transfers between devices: 613 us -> none  [the longest x1 281 us: per_device(): right = lax.psum(partial_right, 'fsdp')]
    pallas_call x0 -> x1, Pallas kernels: none -> 151 us  [per_device(): pl.pallas_call(functools.partial(kernel, nz, nt, factor), out_shape=(jax....]
    all_gather x1 -> x0, waiting for transfers between devices: 145 us -> none  [per_device(): lax.all_gather(basis, 'fsdp', axis=0, tiled=True)]
    another operation x9 -> x0, other arithmetic: 54.5 us -> none  [the longest x6 34 us: orthonormal(): lower = jnp.linalg.cholesky(gram)]
    psum x1 -> x0, blocking collectives: 21 us -> none  [per_device(): squared = lax.psum(jnp.sum(right * right, axis=1), 'tensor')]
    dot_general x5 -> x0, matrix products: 20.8 us -> none  [the longest x1 6.07 us: per_device(): lax.dot_general(blend, lax.all_gather(basis, 'fsdp', axis=0, tiled=True),...]
  transfers between devices with their start and end apart: 4 -> 0, of which waited for: 4 -> 0; matrix products, arithmetic and copies ran while one was open for 0% -> 0% of each run, Pallas kernels for 0% -> 0%
where the time goes in v1:
time: 156 us
  Pallas kernels  151 us (97%)
  local copies, waits for them, and re-layouts  3.73 us (2%)
    pallas_call x1, Pallas kernels, per_device(): pl.pallas_call(functools.partial(kernel, nz, nt, factor), out_shape=(jax....  151 us
    unnamed x4, local copies, waits for them, and re-layouts  3.73 us

profile of v1, /device:TPU:1, one launch (start us, length us, event | category | flops | bytes accessed | tf_op | source)
XLA Modules:
  0.0 155.5 jit_solution(1683969893028771303)
XLA Ops:
  0.6 151.1 %dion_step.1 = (f32[128,3328]{1,0:T(8,128)}, bf16[128,3328]{1,0:T(8,128)(2,1)}) custom-call(f32[128,3328]{1,0:T(8,128)} %mom_hbm.1, bf16[128,3328]{1,0:T(8,128)(2,1)} %grad_hbm.1, f32[1,26,4,128]{3,2,1,0:T(4,128)} %bitcast.3), custom_call_target="tpu_custom_call" | custom-call | tf_op jit(solution)/shard_map/dion_step/pallas_call | solution.py:521
  151.8 0.0 copy-start
  151.8 2.8 %copy.7 = f32[128,3328]{1,0:T(8,128)} copy(f32[128,3328]{1,0:T(8,128)} %get-tuple-element.4) | data formatting | bytes 3407872
  154.6 0.0 copy-done
  154.6 0.9 copy.8
Async XLA Ops:
  151.8 2.8 %copy-start = (bf16[128,3328]{1,0:T(8,128)(2,1)S(1)}, bf16[128,3328]{1,0:T(8,128)(2,1)}, u32[]{:S(2)}) copy-start(bf16[128,3328]{1,0:T(8,128)(2,1)} %get-tuple-element.5) | copy-start | bytes 2555908

commit v2 on v1

--- a/solution.py
+++ b/solution.py
@@ -13,6 +13,7 @@
 NX = 4
 GROUPS = RANK // 4
 PANEL = 32
+MINI = 16
 F32 = jnp.float32
 BF16 = jnp.bfloat16
 HIGHEST = lax.Precision.HIGHEST
@@ -21,6 +22,13 @@
 NN = (((1,), (0,)), ((), ()))
 
 
+def split3(value):
+    high = value.astype(BF16)
+    rest = value - high.astype(F32)
+    mid = rest.astype(BF16)
+    return high, mid, (rest - mid.astype(F32)).astype(BF16)
+
+
 def split(value):
     high = value.astype(BF16)
     return high, (value - high.astype(F32)).astype(BF16)
@@ -43,17 +51,19 @@
     nz, nt, factor,
     mom_hbm, grad_hbm, basis_hbm, newm_hbm, delta_hbm,
     mom, grad, bhi, blo, vbuf, part, proj, rsbuf,
-    wbuf, ropp, rleft, rright, rz, wfin,
+    wbuf, ropp, rleft, rright, rodd, reven, aodd, aeven, across, wfin,
     gram, gslice, grs, gsum, gx, gall, elim,
     rhi, rlo, nbuf, dout,
-    load_sem, store_sem, v_send, v_z, v_l, v_r, v_o,
-    w_send, w_z, w_l, w_r, w_o, r_send, r_z, r_l, r_r, r_o,
+    load_sem, store_sem, v_send, v_z, v_l, v_r, v_o, v_a,
+    w_send, w_z, w_l, w_r, w_o, w_a, r_send, r_odd, r_even, a_odd, a_even, r_l, r_r, r_o,
     s_send, s_recv,
 ):
     rows, cols = mom.shape
     nblk = cols // 128
     nh = nblk // 2
     half = nz // 2
+    na = across.shape[1]
+    nb = nh - na
     m = GROUPS // (nz * NX)
     f = lax.axis_index("fsdp")
     t = lax.axis_index("tensor")
@@ -70,6 +80,7 @@
         return (zz * NX + xx, t)
 
     to_up, to_down = dev(zmod(z + 1), x), dev(zmod(z - 1), x)
+    to_up2, to_down2 = dev(zmod(z + 2), x), dev(zmod(z - 2 + nz), x)
     to_left, to_right, to_opp = dev(z, left), dev(z, right), dev(z, opp)
 
     def remote(src, dst, send, recv, device):
@@ -107,9 +118,35 @@
         greet(device)
     pl.semaphore_wait(barrier, (nz - 1) + (nt - 1) + 3)
 
-    def gather(buf, send, sz, sl, sr, so, early, hook):
+    def gather(buf, cut, send, sz, sl, sr, so, sa, early, hook):
+        whole = buf.shape[1]
+
         def at(zz, xx):
-            return buf.at[pl.ds((zz * NX + xx) * m, m)]
+            return buf.at[pl.ds((zz * NX + xx) * m, m), pl.ds(0, cut)]
+
+        def late(zz, xx):
+            return buf.at[pl.ds((zz * NX + xx) * m, m), pl.ds(cut, whole - cut)]
+
+        def bundle(zz):
+            return buf.at[pl.ds(zz * NX * m, NX * m), pl.ds(cut, whole - cut)]
+
+        def onward(j, ref, sem):
+            @pl.when(j + 1 <= half)
+            def _():
+                remote(ref, ref, send, sem, to_up).start()
+
+            @pl.when(j + 2 <= half)
+            def _():
+                remote(ref, ref, send, sem, to_up2).start()
+
+        def back(j, ref, sem):
+            @pl.when(j + 1 < half)
+            def _():
+                remote(ref, ref, send, sem, to_down).start()
+
+            @pl.when(j + 2 < half)
+            def _():
+                remote(ref, ref, send, sem, to_down2).start()
 
         def push(zz, xx, sem, device):
             remote(at(zz, xx), at(zz, xx), send, sem.at[zz], device).start()
@@ -126,31 +163,50 @@
             wait(at(zz, right), sr.at[zz])
             push(zz, right, so, to_left)
 
-        push(z, x, sz, to_up)
-        if half > 1:
-            push(z, x, sz, to_down)
+        for device in (to_right, to_left, to_opp):
+            remote(late(z, x), late(z, x), send, sa.at[nz], device).start()
+        onward(0, at(z, x), sz.at[z])
+        back(0, at(z, x), sz.at[z])
         spread(z)
         early()
+        wait(buf.at[pl.ds(0, (NX - 1) * m), pl.ds(cut, whole - cut)], sa.at[nz])
+        onward(0, bundle(z), sa.at[z])
+        back(0, bundle(z), sa.at[z])
 
         def step(j, carry):
             below, above = zmod(z - j), zmod(z + j)
+            even = lax.rem(j, 2) == 0
             wait(at(below, x), sz.at[below])
 
+            @pl.when(even)
+            def _():
+                onward(j, at(below, x), sz.at[below])
+
+            spread(below)
+
             @pl.when(j < half)
             def _():
-                push(below, x, sz, to_up)
-
-            spread(below)
+                wait(at(above, x), sz.at[above])
+
+                @pl.when(even)
+                def _():
+                    back(j, at(above, x), sz.at[above])
+
+                spread(above)
+
+            wait(bundle(below), sa.at[below])
+
+            @pl.when(even)
+            def _():
+                onward(j, bundle(below), sa.at[below])
 
             @pl.when(j < half)
             def _():
-                wait(at(above, x), sz.at[above])
-
-                @pl.when(j < half - 1)
+                wait(bundle(above), sa.at[above])
+
+                @pl.when(even)
                 def _():
-                    push(above, x, sz, to_down)
-
-                spread(above)
+                    back(j, bundle(above), sa.at[above])
 
             pass_right(zmod(z - j + 1))
 
@@ -194,7 +250,7 @@
 
         lax.fori_loop(0, nblk // 2, body, 0)
 
-    gather(vbuf, v_send.at[0], v_z, v_l, v_r, v_o, make_blend, lambda j: None)
+    gather(vbuf, 2 * nb, v_send.at[0], v_z, v_l, v_r, v_o, v_a, make_blend, lambda j: None)
 
     def project(c, acc):
         cut = pl.ds(pl.multiple_of(c * 256, 256), 256)
@@ -322,7 +378,16 @@
         return buf.at[pl.ds(index * m, m)]
 
     def wat(q, xx):
-        return piece(wbuf, q * NX + xx)
+        return wbuf.at[pl.ds((q * NX + xx) * m, m), pl.ds(0, nb)]
+
+    def wlate(q, xx):
+        return wbuf.at[pl.ds((q * NX + xx) * m, m), pl.ds(nb, na)]
+
+    def wbundle(q):
+        return wbuf.at[pl.ds(q * NX * m, NX * m), pl.ds(nb, na)]
+
+    def slots(buf, index):
+        return buf.at[pl.ds(index * NX * m, NX * m)]
 
     def add_into(ref, other):
         ref[...] = ref[...] + other[...]
@@ -342,12 +407,70 @@
         here = wat(q, x)
         here[...] = here[...] + (piece(rleft, q)[...] + piece(rright, q)[...])
 
-    def stage_z(q, slot, device):
-        remote(wat(q, x), piece(rz, slot), r_send.at[0], r_z.at[slot], device).start()
-
-    def take_z(q, slot):
-        wait(piece(rz, slot), r_z.at[slot])
-        add_into(wat(q, x), piece(rz, slot))
+    def z_sum(j, top, q, ref, place, odd, even, s_odd, s_even, to_one, to_two, up):
+        def slot(last):
+            return jnp.where(last, nz, q) if up else q
+
+        is_odd = lax.rem(j, 2) == 1
+
+        @pl.when(is_odd & (j <= top))
+        def _():
+            at = slot(j == 1)
+            remote(ref, place(odd, at), r_send.at[0], s_odd.at[at], to_one).start()
+
+        @pl.when(jnp.logical_not(is_odd) & (j >= 2) & (j <= top))
+        def _():
+            @pl.when(j + 1 <= top)
+            def _():
+                wait(place(odd, q), s_odd.at[q])
+                add_into(ref, place(odd, q))
+
+            @pl.when(j + 2 <= top)
+            def _():
+                wait(place(even, q), s_even.at[q])
+                add_into(ref, place(even, q))
+
+            at = slot(j == 2)
+            remote(ref, place(even, at), r_send.at[0], s_even.at[at], to_two).start()
+
+    def z_last(ref, place, odd, even, s_odd, s_even):
+        for buf, sem, index, there in (
+            (odd, s_odd, z, half >= 1), (even, s_even, z, half >= 2),
+            (odd, s_odd, nz, half >= 2), (even, s_even, nz, half >= 3),
+        ):
+            if there:
+                wait(place(buf, index), sem.at[index])
+                add_into(ref, place(buf, index))
+
+    def early_sum(j):
+        args = (slots, aodd, aeven, a_odd, a_even)
+        q = zmod(z - j)
+        z_sum(j, half, q, wbundle(q), *args, to_down, to_down2, False)
+        q = zmod(z + j)
+        z_sum(j, half - 1, q, wbundle(q), *args, to_up, to_up2, True)
+
+        @pl.when(j == 0)
+        def _():
+            z_last(wbundle(z), *args)
+            for xx, device in ((left, to_left), (right, to_right), (opp, to_opp)):
+                remote(wlate(z, xx), piece(across, x), r_send.at[0], a_odd.at[nz + 1], device).start()
+            piece(across, x)[...] = wlate(z, x)[...]
+
+    def late_sum(j):
+        args = (piece, rodd, reven, r_odd, r_even)
+        q = zmod(z - j)
+        stage_c(q)
+        z_sum(j, half, q, wat(q, x), *args, to_down, to_down2, False)
+
+        @pl.when((j >= 1) & (j < half))
+        def _():
+            q = zmod(z + j)
+            stage_c(q)
+            z_sum(j, half - 1, q, wat(q, x), *args, to_up, to_up2, True)
+
+        @pl.when(j == 0)
+        def _():
+            z_last(wat(z, x), *args)
 
     def reduce_step(i, carry):
         @pl.when(i <= half)
@@ -368,36 +491,13 @@
         def _():
             stage_b(zmod(z + half - b), 1)
 
-        c = i - 2
-
-        @pl.when(c >= 0)
-        def _():
-            q = zmod(z - half + c)
-            stage_c(q)
-
-            @pl.when(c > 0)
-            def _():
-                take_z(q, q)
-
-            @pl.when(c < half)
-            def _():
-                stage_z(q, q, to_down)
-
-        @pl.when((c >= 1) & (c < half))
-        def _():
-            q = zmod(z + half - c)
-            stage_c(q)
-
-            @pl.when(c > 1)
-            def _():
-                take_z(q, q)
-
-            stage_z(q, lax.select(c == half - 1, nz, q), to_up)
-
-        if half > 1:
-            @pl.when(c == half)
-            def _():
-                take_z(z, nz)
+        @pl.when(i <= half)
+        def _():
+            early_sum(half - i)
+
+        @pl.when(i >= 2)
+        def _():
+            late_sum(half + 2 - i)
 
         @pl.when(i == max(1, half // 4))
         def _():
@@ -414,7 +514,9 @@
         return carry
 
     lax.fori_loop(0, half + 3, reduce_step, 0)
-    piece(wfin, f)[...] = wat(z, x)[...]
+    wait(across.at[pl.ds(0, (NX - 1) * m)], a_odd.at[nz + 1])
+    wfin[pl.ds(f * m, m), 0:nb] = wat(z, x)[...]
+    wfin[pl.ds(f * m, m), nb:] = jnp.sum(across[...].reshape(NX, m, na, 8, 128), axis=0)
     gram_done()
 
     lane = lax.broadcasted_iota(jnp.int32, (PANEL, 128), 1)
@@ -427,22 +529,33 @@
         block = elim[here, :]
         turned = pltpu.roll(block[:, :RANK], lax.rem(RANK - b * PANEL, RANK), 1)[:, :128]
         state = jnp.where(lane < PANEL, turned, jnp.where(lane == down + PANEL, 1.0, 0.0))
-        for j in range(PANEL - 1):
-            row = state[j : j + 1, :]
-            scale = state[:, j : j + 1] / state[j : j + 1, j : j + 1]
-            state = state - jnp.where(down > j, scale, 0.0) * row
+        for first in range(0, PANEL, MINI):
+            spread = [
+                jnp.broadcast_to(state[:, k : k + 1], (PANEL, 128)) for k in range(first, first + MINI)
+            ]
+            for k in range(min(MINI, PANEL - 1 - first)):
+                j = first + k
+                scale = jnp.where(down > j, spread[k], 0.0) * (1.0 / spread[k][j : j + 1, :])
+                state = state - scale * state[j : j + 1, :]
+                for n in range(k + 1, MINI):
+                    spread[n] = spread[n] - scale * spread[n][j : j + 1, :]
         diag = jnp.sum(jnp.where(lane == down, state, 0.0), axis=1, keepdims=True)
         lower = state[:, PANEL : 2 * PANEL] / jnp.sqrt(diag)
         done = dot_full(lower, block, NN)
         rest = jnp.where(wide >= (b + 1) * PANEL, done[:, :RANK], 0.0)
-        elim[...] = elim[...] - dot_full(rest, done, TN)
+        (rh, rm, rl), (dh, dm, dl) = split3(rest), split3(done)
+        elim[...] = elim[...] - dot(
+            jnp.concatenate([rh, rh, rh, rm, rm, rl], axis=0),
+            jnp.concatenate([dh, dm, dl, dh, dm, dh], axis=0),
+            TN,
+        )
         elim[here, :] = done
 
     def panels(j):
         for k in range(npanel // half):
             panel((j - 1) * (npanel // half) + k)
 
-    gather(wfin, w_send.at[0], w_z, w_l, w_r, w_o, lambda: None, panels)
+    gather(wfin, nb, w_send.at[0], w_z, w_l, w_r, w_o, w_a, lambda: None, panels)
     wait(wbuf.at[pl.ds(0, (nz * NX - 1) * m)], r_send.at[0])
 
     inv_lower = elim[:, RANK:]
@@ -513,6 +626,8 @@
     gshare = RANK // nt
     ng = 2 * gshare // 4
     mg = ng // nz
+    na = max(1, nh // 4)
+    nb = nh - na
     tiles = basis.reshape(m, 4, nblk, 128).transpose(0, 2, 1, 3)
     vmem = pltpu.VMEM
     dma = pltpu.SemaphoreType.DMA
@@ -536,10 +651,14 @@
             vmem((rows, RANK), F32),
             vmem((one, rows // nt, RANK), F32),
             vmem((GROUPS, nh, 8, 128), F32),
-            vmem((nz * m, nh, 8, 128), F32),
-            vmem((nz * m, nh, 8, 128), F32),
-            vmem((nz * m, nh, 8, 128), F32),
-            vmem(((nz + 1) * m, nh, 8, 128), F32),
+            vmem((nz * m, nb, 8, 128), F32),
+            vmem((nz * m, nb, 8, 128), F32),
+            vmem((nz * m, nb, 8, 128), F32),
+            vmem(((nz + 1) * m, nb, 8, 128), F32),
+            vmem(((nz + 1) * m, nb, 8, 128), F32),
+            vmem(((nz + 1) * NX * m, na, 8, 128), F32),
+            vmem(((nz + 1) * NX * m, na, 8, 128), F32),
+            vmem((NX * m, na, 8, 128), F32),
             vmem((GROUPS, nh, 8, 128), F32),
             vmem((RANK, RANK), F32),
             vmem((ng, 4, 128), F32),
@@ -554,9 +673,10 @@
             vmem((rows, cols), BF16),
             dma((3,)),
             dma((16,)),
-            dma((1,)), dma((nz,)), dma((nz,)), dma((nz,)), dma((nz,)),
-            dma((1,)), dma((nz,)), dma((nz,)), dma((nz,)), dma((nz,)),
-            dma((1,)), dma((nz + 1,)), dma((nz,)), dma((nz,)), dma((nz,)),
+            dma((1,)), dma((nz,)), dma((nz,)), dma((nz,)), dma((nz,)), dma((nz + 1,)),
+            dma((1,)), dma((nz,)), dma((nz,)), dma((nz,)), dma((nz,)), dma((nz + 1,)),
+            dma((1,)), dma((nz + 1,)), dma((nz + 1,)), dma((nz + 2,)), dma((nz + 1,)),
+            dma((nz,)), dma((nz,)), dma((nz,)),
             dma((7,)),
             dma((7,)),
         ],

time: 156 us -> 153 us (0.981)
  Pallas kernels: 151 us -> 149 us
    pallas_call x1, Pallas kernels: 151 us -> 149 us  [per_device(): pl.pallas_call(functools.partial(kernel, nz, nt, factor), out_shape=(jax....]
where the time goes in v2:
time: 153 us
  Pallas kernels  149 us (97%)
  local copies, waits for them, and re-layouts  3.73 us (2%)
    pallas_call x1, Pallas kernels, per_device(): pl.pallas_call(functools.partial(kernel, nz, nt, factor), out_shape=(jax....  149 us
    unnamed x4, local copies, waits for them, and re-layouts  3.73 us

profile of v2, /device:TPU:1, one launch (start us, length us, event | category | flops | bytes accessed | tf_op | source)
XLA Modules:
  0.0 153.0 jit_solution(12748529078423440722)
XLA Ops:
  0.6 148.6 %dion_step.1 = (f32[128,3328]{1,0:T(8,128)}, bf16[128,3328]{1,0:T(8,128)(2,1)}) custom-call(f32[128,3328]{1,0:T(8,128)} %mom_hbm.1, bf16[128,3328]{1,0:T(8,128)(2,1)} %grad_hbm.1, f32[1,26,4,128]{3,2,1,0:T(4,128)} %bitcast.3), custom_call_target="tpu_custom_call" | custom-call | tf_op jit(solution)/shard_map/dion_step/pallas_call | solution.py:636
  149.3 0.0 copy-start
  149.3 2.8 %copy.7 = f32[128,3328]{1,0:T(8,128)} copy(f32[128,3328]{1,0:T(8,128)} %get-tuple-element.4) | data formatting | bytes 3407872
  152.1 0.0 copy-done
  152.1 0.9 copy.8
Async XLA Ops:
  149.3 2.8 %copy-start = (bf16[128,3328]{1,0:T(8,128)(2,1)S(1)}, bf16[128,3328]{1,0:T(8,128)(2,1)}, u32[]{:S(2)}) copy-start(bf16[128,3328]{1,0:T(8,128)(2,1)} %get-tuple-element.5) | copy-start | bytes 2555908

commit v3 on v2

--- a/solution.py
+++ b/solution.py
@@ -14,6 +14,11 @@
 GROUPS = RANK // 4
 PANEL = 32
 MINI = 16
+NA = 2
+LAG = 2
+LAG_B = 2
+LAG_C = 4
+GRAM_AT = (2, 4, 6, 9)
 F32 = jnp.float32
 BF16 = jnp.bfloat16
 HIGHEST = lax.Precision.HIGHEST
@@ -47,13 +52,24 @@
     return lax.dot_general(a, b, dims, precision=HIGHEST, preferred_element_type=F32)
 
 
+def cuts_of(nh):
+    cuts = []
+    for h in range(2):
+        start = 0
+        while start < nh:
+            width = min(4, nh - start) if nh - start != 5 else 5
+            cuts.append((h, start, width))
+            start += width
+    return cuts
+
+
 def kernel(
     nz, nt, factor,
-    mom_hbm, grad_hbm, basis_hbm, newm_hbm, delta_hbm,
+    mom_hbm, grad_hbm, basis_hbm, high_hbm, low_hbm, ortho_out, scaled_high, scaled_low,
     mom, grad, bhi, blo, vbuf, part, proj, rsbuf,
     wbuf, ropp, rleft, rright, rodd, reven, aodd, aeven, across, wfin,
     gram, gslice, grs, gsum, gx, gall, elim,
-    rhi, rlo, nbuf, dout,
+    rhi, rlo, nbuf,
     load_sem, store_sem, v_send, v_z, v_l, v_r, v_o, v_a,
     w_send, w_z, w_l, w_r, w_o, w_a, r_send, r_odd, r_even, a_odd, a_even, r_l, r_r, r_o,
     s_send, s_recv,
@@ -104,19 +120,16 @@
     def greet(device):
         pl.semaphore_signal(barrier, inc=1, device_id=device, device_id_type=pl.DeviceIdType.MESH)
 
-    def greet_z(r, carry):
-        greet(dev(zmod(z + r), x))
-        return carry
-
     def greet_t(r, carry):
         greet((f, tmod(t + r)))
         return carry
 
-    lax.fori_loop(1, nz, greet_z, 0)
     lax.fori_loop(1, nt, greet_t, 0)
-    for device in (to_left, to_right, to_opp):
+    near = [to_left, to_right, to_opp]
+    near += [dev(zmod(z + r), x) for r in sorted({1 % nz, nz - 1, 2 % nz, nz - 2} - {0})]
+    for device in near:
         greet(device)
-    pl.semaphore_wait(barrier, (nz - 1) + (nt - 1) + 3)
+    pl.semaphore_wait(barrier, (nt - 1) + len(near))
 
     def gather(buf, cut, send, sz, sl, sr, so, sa, early, hook):
         whole = buf.shape[1]
@@ -131,22 +144,22 @@
             return buf.at[pl.ds(zz * NX * m, NX * m), pl.ds(cut, whole - cut)]
 
         def onward(j, ref, sem):
+            @pl.when(j + 2 <= half)
+            def _():
+                remote(ref, ref, send, sem, to_up2).start()
+
             @pl.when(j + 1 <= half)
             def _():
                 remote(ref, ref, send, sem, to_up).start()
 
-            @pl.when(j + 2 <= half)
-            def _():
-                remote(ref, ref, send, sem, to_up2).start()
-
         def back(j, ref, sem):
+            @pl.when(j + 2 < half)
+            def _():
+                remote(ref, ref, send, sem, to_down2).start()
+
             @pl.when(j + 1 < half)
             def _():
                 remote(ref, ref, send, sem, to_down).start()
-
-            @pl.when(j + 2 < half)
-            def _():
-                remote(ref, ref, send, sem, to_down2).start()
 
         def push(zz, xx, sem, device):
             remote(at(zz, xx), at(zz, xx), send, sem.at[zz], device).start()
@@ -162,6 +175,15 @@
         def pass_left(zz):
             wait(at(zz, right), sr.at[zz])
             push(zz, right, so, to_left)
+
+        def passing(j):
+            @pl.when(j >= 0)
+            def _():
+                pass_right(zmod(z - j))
+
+            @pl.when((j > 0) & (j < half))
+            def _():
+                pass_left(zmod(z + j))
 
         for device in (to_right, to_left, to_opp):
             remote(late(z, x), late(z, x), send, sa.at[nz], device).start()
@@ -176,13 +198,26 @@
         def step(j, carry):
             below, above = zmod(z - j), zmod(z + j)
             even = lax.rem(j, 2) == 0
+            def late_ones():
+                wait(bundle(below), sa.at[below])
+
+                @pl.when(even)
+                def _():
+                    onward(j, bundle(below), sa.at[below])
+
+                @pl.when(j < half)
+                def _():
+                    wait(bundle(above), sa.at[above])
+
+                    @pl.when(even)
+                    def _():
+                        back(j, bundle(above), sa.at[above])
+
             wait(at(below, x), sz.at[below])
 
             @pl.when(even)
             def _():
                 onward(j, at(below, x), sz.at[below])
-
-            spread(below)
 
             @pl.when(j < half)
             def _():
@@ -192,33 +227,19 @@
                 def _():
                     back(j, at(above, x), sz.at[above])
 
+            spread(below)
+
+            @pl.when(j < half)
+            def _():
                 spread(above)
 
-            wait(bundle(below), sa.at[below])
-
-            @pl.when(even)
-            def _():
-                onward(j, bundle(below), sa.at[below])
-
-            @pl.when(j < half)
-            def _():
-                wait(bundle(above), sa.at[above])
-
-                @pl.when(even)
-                def _():
-                    back(j, bundle(above), sa.at[above])
-
-            pass_right(zmod(z - j + 1))
-
-            @pl.when(j > 1)
-            def _():
-                pass_left(zmod(z + j - 1))
-
+            late_ones()
+            passing(j - LAG)
             hook(j)
             return carry
 
         lax.fori_loop(1, half + 1, step, 0)
-        pass_right(zmod(z - half))
+        lax.fori_loop(half + 1 - LAG, half + 1, lambda j, carry: (passing(j), carry)[1], 0)
 
         def finish(j, carry):
             below, above = zmod(z - j), zmod(z + j)
@@ -363,16 +384,12 @@
     gram_send()
 
     turned = split(full.T)
-    for h in range(2):
-        start = 0
-        while start < nh:
-            width = min(4, nh - start) if nh - start != 5 else 5
-            cut = slice((h * nh + start) * 128, (h * nh + start + width) * 128)
-            out = dot3(turned, (bhi[:, cut], blo[:, cut]), NN)
-            for k in range(width):
-                for r in range(RANK // 8):
-                    wbuf[2 * r + h, start + k] = out[8 * r : 8 * r + 8, 128 * k : 128 * k + 128]
-            start += width
+    for h, start, width in cuts_of(nh):
+        cut = slice((h * nh + start) * 128, (h * nh + start + width) * 128)
+        out = dot3(turned, (bhi[:, cut], blo[:, cut]), NN)
+        for k in range(width):
+            for r in range(RANK // 8):
+                wbuf[2 * r + h, start + k] = out[8 * r : 8 * r + 8, 128 * k : 128 * k + 128]
 
     def piece(buf, index):
         return buf.at[pl.ds(index * m, m)]
@@ -471,53 +488,6 @@
         @pl.when(j == 0)
         def _():
             z_last(wat(z, x), *args)
-
-    def reduce_step(i, carry):
-        @pl.when(i <= half)
-        def _():
-            stage_a(zmod(z - half + i), 0)
-
-        @pl.when((i >= 1) & (i < half))
-        def _():
-            stage_a(zmod(z + half - i), 1)
-
-        b = i - 1
-
-        @pl.when((b >= 0) & (b <= half))
-        def _():
-            stage_b(zmod(z - half + b), 0)
-
-        @pl.when((b >= 1) & (b < half))
-        def _():
-            stage_b(zmod(z + half - b), 1)
-
-        @pl.when(i <= half)
-        def _():
-            early_sum(half - i)
-
-        @pl.when(i >= 2)
-        def _():
-            late_sum(half + 2 - i)
-
-        @pl.when(i == max(1, half // 4))
-        def _():
-            gram_over_z()
-
-        @pl.when(i == max(2, half // 2))
-        def _():
-            gram_over_x()
-
-        @pl.when(i == max(3, 3 * half // 4))
-        def _():
-            gram_over_t()
-
-        return carry
-
-    lax.fori_loop(0, half + 3, reduce_step, 0)
-    wait(across.at[pl.ds(0, (NX - 1) * m)], a_odd.at[nz + 1])
-    wfin[pl.ds(f * m, m), 0:nb] = wat(z, x)[...]
-    wfin[pl.ds(f * m, m), nb:] = jnp.sum(across[...].reshape(NX, m, na, 8, 128), axis=0)
-    gram_done()
 
     lane = lax.broadcasted_iota(jnp.int32, (PANEL, 128), 1)
     down = lax.broadcasted_iota(jnp.int32, (PANEL, 128), 0)
@@ -551,9 +521,54 @@
         )
         elim[here, :] = done
 
+    def reduce_step(i, carry):
+        @pl.when(i <= half)
+        def _():
+            stage_a(zmod(z - half + i), 0)
+
+        @pl.when((i >= 1) & (i < half))
+        def _():
+            stage_a(zmod(z + half - i), 1)
+
+        b = i - LAG_B
+
+        @pl.when((b >= 0) & (b <= half))
+        def _():
+            stage_b(zmod(z - half + b), 0)
+
+        @pl.when((b >= 1) & (b < half))
+        def _():
+            stage_b(zmod(z + half - b), 1)
+
+        @pl.when(i <= half)
+        def _():
+            early_sum(half - i)
+
+        @pl.when(i >= LAG_C)
+        def _():
+            late_sum(half + LAG_C - i)
+
+        last = half + LAG_C
+        for place, work in zip(GRAM_AT, (gram_over_z, gram_over_x, gram_over_t, gram_done)):
+            pl.when(i == min(place, last))(work)
+
+        @pl.when(i > max(GRAM_AT))
+        def _():
+            panel(i - max(GRAM_AT) - 1)
+
+        return carry
+
+    lax.fori_loop(0, half + 1 + LAG_C, reduce_step, 0)
+    wait(across.at[pl.ds(0, (NX - 1) * m)], a_odd.at[nz + 1])
+    wfin[pl.ds(f * m, m), 0:nb] = wat(z, x)[...]
+    wfin[pl.ds(f * m, m), nb:] = jnp.sum(across[...].reshape(NX, m, na, 8, 128), axis=0)
+
+    begun = max(0, half + LAG_C - max(GRAM_AT))
+
     def panels(j):
-        for k in range(npanel // half):
-            panel((j - 1) * (npanel // half) + k)
+        for k in range(-(-(npanel - begun) // half)):
+            b = begun + (j - 1) * (-(-(npanel - begun) // half)) + k
+            pl.when(b < npanel)(functools.partial(panel, b))
 
     gather(wfin, nb, w_send.at[0], w_z, w_l, w_r, w_o, w_a, lambda: None, panels)
     wait(wbuf.at[pl.ds(0, (nz * NX - 1) * m)], r_send.at[0])
@@ -562,14 +577,8 @@
     ortho = dot_full(proj[...], inv_lower, NT)
     low = split(inv_lower)
     squared = jnp.zeros((RANK, 128), F32)
-    cuts = []
-    for h in range(2):
-        start = 0
-        while start < nh:
-            width = min(4, nh - start) if nh - start != 5 else 5
-            cuts.append((h, start, width))
-            start += width
-    for h, start, width in cuts:
+    stores = []
+    for n, (h, start, width) in enumerate(cuts_of(nh)):
         cut = slice((h * nh + start) * 128, (h * nh + start + width) * 128)
         columns = [
             jnp.concatenate([wfin[2 * r + h, start + k] for r in range(RANK // 8)], axis=0)
@@ -580,6 +589,9 @@
             one = out[:, 128 * k : 128 * k + 128]
             squared = squared + one * one
         rhi[:, cut], rlo[:, cut] = split(out)
+        for k, (buf, hbm) in enumerate(((rhi, high_hbm), (rlo, low_hbm))):
+            stores.append(pltpu.make_async_copy(buf.at[:, cut], hbm.at[:, cut], store_sem.at[2 * n + k]))
+            stores[-1].start()
     nbuf[t] = dot_full(jnp.ones((8, 128), F32), squared, NT)
 
     if nt > 1:
@@ -591,14 +603,7 @@
 
         lax.fori_loop(1, nt, send_norm, 0)
 
-    ortho_high = ortho.astype(BF16)
-    stores = []
-    for n, (h, start, width) in enumerate(cuts):
-        cut = slice((h * nh + start) * 128, (h * nh + start + width) * 128)
-        mom[:, cut] = mom[:, cut] - 0.05 * dot(ortho_high, rhi[:, cut], NN)
-        stores.append(pltpu.make_async_copy(mom.at[:, cut], newm_hbm.at[:, cut], store_sem.at[n]))
-        stores[-1].start()
-
+    ortho_out[...] = ortho.astype(BF16)
     if nt > 1:
         wait(nbuf.at[pl.ds(0, nt - 1)], s_recv.at[6])
         wait(nbuf.at[pl.ds(0, nt - 1)], s_send.at[6])
@@ -606,14 +611,37 @@
     for r in range(1, nt):
         norm = norm + nbuf[r]
     inverse = 1.0 / (jnp.sqrt(norm) + 1e-06)
-    scaled = split(ortho * (inverse[0:1, :] * -factor))
+    scaled_high[...], scaled_low[...] = split(ortho * (inverse[0:1, :] * -factor))
+    for store in stores:
+        store.wait()
+
+
+def update(
+    mom_hbm, grad_hbm, high_hbm, low_hbm, ortho, scaled_high, scaled_low, newm_hbm, delta_hbm,
+    mom, grad, rhi, rlo, dout, load_sem, store_sem,
+):
+    cuts = cuts_of(mom.shape[1] // 256)
+    nh = mom.shape[1] // 256
+    pairs = ((high_hbm, rhi), (low_hbm, rlo), (mom_hbm, mom), (grad_hbm, grad))
+    loads, stores = [], []
     for n, (h, start, width) in enumerate(cuts):
         cut = slice((h * nh + start) * 128, (h * nh + start + width) * 128)
-        dout[:, cut] = dot3(scaled, (rhi[:, cut], rlo[:, cut]), NN).astype(BF16)
-        stores.append(
-            pltpu.make_async_copy(dout.at[:, cut], delta_hbm.at[:, cut], store_sem.at[len(cuts) + n])
-        )
-        stores[-1].start()
+        for k, (hbm, buf) in enumerate(pairs):
+            loads.append(pltpu.make_async_copy(hbm.at[:, cut], buf.at[:, cut], load_sem.at[4 * n + k]))
+            loads[-1].start()
+    both = jnp.concatenate([scaled_high[...], scaled_low[...], ortho[...]], axis=0)
+    rows = ortho.shape[0]
+    for n, (h, start, width) in enumerate(cuts):
+        cut = slice((h * nh + start) * 128, (h * nh + start + width) * 128)
+        for load in loads[4 * n : 4 * n + 4]:
+            load.wait()
+        high = dot(both, rhi[:, cut], NN)
+        delta = high[:rows] + (high[rows : 2 * rows] + dot(scaled_high[...], rlo[:, cut], NN))
+        dout[:, cut] = delta.astype(BF16)
+        mom[:, cut] = (mom[:, cut] + grad[:, cut].astype(F32)) - 0.05 * high[2 * rows :]
+        for k, (buf, hbm) in enumerate(((mom, newm_hbm), (dout, delta_hbm))):
+            stores.append(pltpu.make_async_copy(buf.at[:, cut], hbm.at[:, cut], store_sem.at[2 * n + k]))
+            stores[-1].start()
     for store in stores:
         store.wait()
 
@@ -626,21 +654,26 @@
     gshare = RANK // nt
     ng = 2 * gshare // 4
     mg = ng // nz
-    na = max(1, nh // 4)
+    na = min(NA, nh - 1)
     nb = nh - na
     tiles = basis.reshape(m, 4, nblk, 128).transpose(0, 2, 1, 3)
     vmem = pltpu.VMEM
     dma = pltpu.SemaphoreType.DMA
     any_spec = pl.BlockSpec(memory_space=pl.ANY)
     one = max(nt - 1, 1)
-    return pl.pallas_call(
+    vmem_spec = pl.BlockSpec(memory_space=pltpu.VMEM)
+    ncut = len(cuts_of(nh))
+    high, low, ortho, scaled_high, scaled_low = pl.pallas_call(
         functools.partial(kernel, nz, nt, factor),
         out_shape=(
-            jax.ShapeDtypeStruct((rows, cols), F32),
-            jax.ShapeDtypeStruct((rows, cols), BF16),
+            jax.ShapeDtypeStruct((RANK, cols), BF16),
+            jax.ShapeDtypeStruct((RANK, cols), BF16),
+            jax.ShapeDtypeStruct((rows, RANK), BF16),
+            jax.ShapeDtypeStruct((rows, RANK), BF16),
+            jax.ShapeDtypeStruct((rows, RANK), BF16),
         ),
         in_specs=[any_spec] * 3,
-        out_specs=(any_spec, any_spec),
+        out_specs=(any_spec, any_spec, vmem_spec, vmem_spec, vmem_spec),
         scratch_shapes=[
             vmem((rows, cols), F32),
             vmem((rows, cols), BF16),
@@ -670,9 +703,8 @@
             vmem((RANK, cols), BF16),
             vmem((RANK, cols), BF16),
             vmem((nt, 8, RANK), F32),
-            vmem((rows, cols), BF16),
             dma((3,)),
-            dma((16,)),
+            dma((2 * ncut,)),
             dma((1,)), dma((nz,)), dma((nz,)), dma((nz,)), dma((nz,)), dma((nz + 1,)),
             dma((1,)), dma((nz,)), dma((nz,)), dma((nz,)), dma((nz,)), dma((nz + 1,)),
             dma((1,)), dma((nz + 1,)), dma((nz + 1,)), dma((nz + 2,)), dma((nz + 1,)),
@@ -685,6 +717,26 @@
         ),
         name="dion_step",
     )(momentum, gradient, tiles)
+    return pl.pallas_call(
+        update,
+        out_shape=(
+            jax.ShapeDtypeStruct((rows, cols), F32),
+            jax.ShapeDtypeStruct((rows, cols), BF16),
+        ),
+        in_specs=[any_spec] * 4 + [vmem_spec] * 3,
+        out_specs=(any_spec, any_spec),
+        scratch_shapes=[
+            vmem((rows, cols), F32),
+            vmem((rows, cols), BF16),
+            vmem((RANK, cols), BF16),
+            vmem((RANK, cols), BF16),
+            vmem((rows, cols), BF16),
+            dma((4 * ncut,)),
+            dma((2 * ncut,)),
+        ],
+        compiler_params=pltpu.CompilerParams(vmem_limit_bytes=56 * 2**20),
+        name="dion_update",
+    )(momentum, gradient, high, low, ortho, scaled_high, scaled_low)
 
 
 def solution(mesh):

time: 153 us -> 152 us (level)
  local copies, waits for them, and re-layouts: 3.73 us -> 0 us
  Pallas kernels: 149 us -> 151 us
    pallas_call x0 -> x1, Pallas kernels: none -> 5.34 us  [per_device(): pl.pallas_call(update, out_shape=(jax.ShapeDtypeStruct((rows, cols), F32)...]
    unnamed x4 -> x0, local copies, waits for them, and re-layouts: 3.73 us -> none
    pallas_call x1, Pallas kernels: 149 us -> 146 us  [per_device(): pl.pallas_call(functools.partial(kernel, nz, nt, factor), out_shape=(jax....]
where the time goes in v3:
time: 152 us
  Pallas kernels  151 us (99%)
    pallas_call x1, Pallas kernels, per_device(): pl.pallas_call(functools.partial(kernel, nz, nt, factor), out_shape=(jax....  146 us
    pallas_call x1, Pallas kernels, per_device(): pl.pallas_call(update, out_shape=(jax.ShapeDtypeStruct((rows, cols), F32)...  5.34 us

profile of v3, /device:TPU:1, one launch (start us, length us, event | category | flops | bytes accessed | tf_op | source)
XLA Modules:
  0.0 151.7 jit_solution(6265819852742687503)
XLA Ops:
  0.6 145.7 %dion_step.1 = (bf16[256,3328]{1,0:T(8,128)(2,1)}, bf16[256,3328]{1,0:T(8,128)(2,1)}, bf16[128,256]{1,0:T(8,128)(2,1)}, bf16[128,256]{1,0:T(8,128)(2,1)}, bf16[128,256]{1,0:T(8,128)(2,1)}) custom-call(f32[128,3328]{1,0:T(8,128)} %mom_hbm.3, bf16[128,3328]{1,0:T(8,128)(2,1)} %grad_hbm.3, f32[1,26,4,128]{3,2,1,0:T(4,128)} %bitcast.3), custom_call_target="tpu_custom_call" | custom-call | tf_op jit(solution)/shard_map/dion_step/pallas_call | solution.py:666
  146.3 5.3 %dion_update.1 = (f32[128,3328]{1,0:T(8,128)}, bf16[128,3328]{1,0:T(8,128)(2,1)}) custom-call(f32[128,3328]{1,0:T(8,128)} %mom_hbm.3, bf16[128,3328]{1,0:T(8,128)(2,1)} %grad_hbm.3, bf16[256,3328]{1,0:T(8,128)(2,1)} %get-tuple-element.7.high_hbm, bf16[256,3328]{1,0:T(8,128)(2,1)} %get-tuple-element.8.low_hbm, bf16[128,256]{1,0:T(8,128)(2,1)} %get-tuple-element.9.ortho, ...), custom_call_target="tpu_custom_call" | custom-call | tf_op jit(solution)/shard_map/dion_update/pallas_call | solution.py:720

commit v4 on v3

--- a/solution.py
+++ b/solution.py
@@ -16,6 +16,9 @@
 MINI = 16
 NA = 2
 LAG = 2
+LAG_A = 2
+UNROLL = 13
+LAG_S = 1
 LAG_B = 2
 LAG_C = 4
 GRAM_AT = (2, 4, 6, 9)
@@ -176,8 +179,22 @@
             wait(at(zz, right), sr.at[zz])
             push(zz, right, so, to_left)
 
+        def late_ones(j):
+            below, above = zmod(z - j), zmod(z + j)
+            even = lax.rem(j, 2) == 0
+
+            @pl.when((j > 0) & (j <= half))
+            def _():
+                wait(bundle(below), sa.at[below])
+                pl.when(even)(lambda: onward(j, bundle(below), sa.at[below]))
+
+            @pl.when((j > 0) & (j < half))
+            def _():
+                wait(bundle(above), sa.at[above])
+                pl.when(even)(lambda: back(j, bundle(above), sa.at[above]))
+
         def passing(j):
-            @pl.when(j >= 0)
+            @pl.when((j >= 0) & (j <= half))
             def _():
                 pass_right(zmod(z - j))
 
@@ -198,21 +215,6 @@
         def step(j, carry):
             below, above = zmod(z - j), zmod(z + j)
             even = lax.rem(j, 2) == 0
-            def late_ones():
-                wait(bundle(below), sa.at[below])
-
-                @pl.when(even)
-                def _():
-                    onward(j, bundle(below), sa.at[below])
-
-                @pl.when(j < half)
-                def _():
-                    wait(bundle(above), sa.at[above])
-
-                    @pl.when(even)
-                    def _():
-                        back(j, bundle(above), sa.at[above])
-
             wait(at(below, x), sz.at[below])
 
             @pl.when(even)
@@ -233,13 +235,20 @@
             def _():
                 spread(above)
 
-            late_ones()
+            late_ones(j - LAG_A)
             passing(j - LAG)
             hook(j)
             return carry
 
         lax.fori_loop(1, half + 1, step, 0)
-        lax.fori_loop(half + 1 - LAG, half + 1, lambda j, carry: (passing(j), carry)[1], 0)
+        rest = max(LAG, LAG_A)
+
+        def drain(j, carry):
+            late_ones(j - LAG_A)
+            passing(j - LAG)
+            return carry
+
+        lax.fori_loop(half + 1, half + 1 + rest, drain, 0)
 
         def finish(j, carry):
             below, above = zmod(z - j), zmod(z + j)
@@ -278,7 +287,7 @@
         pair = [vbuf[:, 2 * c + k].reshape(RANK, 128) for k in range(2)]
         return acc + dot3((bhi[:, cut], blo[:, cut]), split(jnp.concatenate(pair, axis=1)), NT)
 
-    part[...] = lax.fori_loop(0, nblk // 2, project, jnp.zeros((rows, RANK), F32))
+    part[...] = lax.fori_loop(0, nblk // 2, project, jnp.zeros((rows, RANK), F32), unroll=UNROLL)
 
     share = rows // nt
     if nt > 1:
@@ -540,9 +549,9 @@
         def _():
             stage_b(zmod(z + half - b), 1)
 
-        @pl.when(i <= half)
-        def _():
-            early_sum(half - i)
+        @pl.when((i >= LAG_S) & (i <= half + LAG_S))
+        def _():
+            early_sum(half + LAG_S - i)
 
         @pl.when(i >= LAG_C)
         def _():
@@ -566,9 +575,13 @@
     begun = max(0, half + LAG_C - max(GRAM_AT))
 
     def panels(j):
-        for k in range(-(-(npanel - begun) // half)):
-            b = begun + (j - 1) * (-(-(npanel - begun) // half)) + k
-            pl.when(b < npanel)(functools.partial(panel, b))
+        per = -(-(npanel - begun) // max(half // 2, 1))
+
+        @pl.when(lax.rem(j, 2) == (0 if half > 1 else 1))
+        def _():
+            for k in range(per):
+                b = begun + (lax.div(j, 2) - (1 if half > 1 else 0)) * per + k
+                pl.when(b < npanel)(functools.partial(panel, b))
 
     gather(wfin, nb, w_send.at[0], w_z, w_l, w_r, w_o, w_a, lambda: None, panels)
     wait(wbuf.at[pl.ds(0, (nz * NX - 1) * m)], r_send.at[0])

time: 152 us -> 141 us (0.928)
  Pallas kernels: 151 us -> 140 us
    pallas_call x1, Pallas kernels: 146 us -> 135 us  [per_device(): pl.pallas_call(functools.partial(kernel, nz, nt, factor), out_shape=(jax....]
where the time goes in v4:
time: 141 us
  Pallas kernels  140 us (99%)
    pallas_call x1, Pallas kernels, per_device(): pl.pallas_call(functools.partial(kernel, nz, nt, factor), out_shape=(jax....  135 us
    pallas_call x1, Pallas kernels, per_device(): pl.pallas_call(update, out_shape=(jax.ShapeDtypeStruct((rows, cols), F32)...  5.34 us

profile of v4, /device:TPU:1, one launch (start us, length us, event | category | flops | bytes accessed | tf_op | source)
XLA Modules:
  0.0 140.8 jit_solution(5437237280941885706)
XLA Ops:
  0.6 134.8 %dion_step.1 = (bf16[256,3328]{1,0:T(8,128)(2,1)}, bf16[256,3328]{1,0:T(8,128)(2,1)}, bf16[128,256]{1,0:T(8,128)(2,1)}, bf16[128,256]{1,0:T(8,128)(2,1)}, bf16[128,256]{1,0:T(8,128)(2,1)}) custom-call(f32[128,3328]{1,0:T(8,128)} %mom_hbm.3, bf16[128,3328]{1,0:T(8,128)(2,1)} %grad_hbm.3, f32[1,26,4,128]{3,2,1,0:T(4,128)} %bitcast.3), custom_call_target="tpu_custom_call" | custom-call | tf_op jit(solution)/shard_map/dion_step/pallas_call | solution.py:679
  135.5 5.3 %dion_update.1 = (f32[128,3328]{1,0:T(8,128)}, bf16[128,3328]{1,0:T(8,128)(2,1)}) custom-call(f32[128,3328]{1,0:T(8,128)} %mom_hbm.3, bf16[128,3328]{1,0:T(8,128)(2,1)} %grad_hbm.3, bf16[256,3328]{1,0:T(8,128)(2,1)} %get-tuple-element.7.high_hbm, bf16[256,3328]{1,0:T(8,128)(2,1)} %get-tuple-element.8.low_hbm, bf16[128,256]{1,0:T(8,128)(2,1)} %get-tuple-element.9.ortho, ...), custom_call_target="tpu_custom_call" | custom-call | tf_op jit(solution)/shard_map/dion_update/pallas_call | solution.py:733

commit v5 on v4

--- a/solution.py
+++ b/solution.py
@@ -19,8 +19,8 @@
 LAG_A = 2
 UNROLL = 13
 LAG_S = 1
-LAG_B = 2
-LAG_C = 4
+LAG_B = 1
+LAG_C = 3
 GRAM_AT = (2, 4, 6, 9)
 F32 = jnp.float32
 BF16 = jnp.bfloat16
@@ -72,7 +72,7 @@
     mom, grad, bhi, blo, vbuf, part, proj, rsbuf,
     wbuf, ropp, rleft, rright, rodd, reven, aodd, aeven, across, wfin,
     gram, gslice, grs, gsum, gx, gall, elim,
-    rhi, rlo, nbuf,
+    rhi, rlo, nbuf, ortho_f32, lhi, llo,
     load_sem, store_sem, v_send, v_z, v_l, v_r, v_o, v_a,
     w_send, w_z, w_l, w_r, w_o, w_a, r_send, r_odd, r_even, a_odd, a_even, r_l, r_r, r_o,
     s_send, s_recv,
@@ -134,7 +134,7 @@
         greet(device)
     pl.semaphore_wait(barrier, (nt - 1) + len(near))
 
-    def gather(buf, cut, send, sz, sl, sr, so, sa, early, hook):
+    def gather(buf, cut, send, sz, sl, sr, so, sa, early, hook, tail):
         whole = buf.shape[1]
 
         def at(zz, xx):
@@ -194,12 +194,13 @@
                 pl.when(even)(lambda: back(j, bundle(above), sa.at[above]))
 
         def passing(j):
-            @pl.when((j >= 0) & (j <= half))
+            @pl.when(j == 0)
+            def _():
+                pass_left(z)
+
+            @pl.when((j > 0) & (j < half))
             def _():
                 pass_right(zmod(z - j))
-
-            @pl.when((j > 0) & (j < half))
-            def _():
                 pass_left(zmod(z + j))
 
         for device in (to_right, to_left, to_opp):
@@ -235,6 +236,7 @@
             def _():
                 spread(above)
 
+            pl.when(j == half)(lambda: push(below, x, so, to_opp))
             late_ones(j - LAG_A)
             passing(j - LAG)
             hook(j)
@@ -252,8 +254,9 @@
 
         def finish(j, carry):
             below, above = zmod(z - j), zmod(z + j)
-            wait(at(below, right), sr.at[below])
             wait(at(below, opp), so.at[below])
+            pl.when(j > 0)(lambda: wait(at(below, right), sr.at[below]))
+            pl.when((j == 0) | (j == half))(lambda: wait(at(below, left), sl.at[below]))
 
             @pl.when((j > 0) & (j < half))
             def _():
@@ -262,8 +265,8 @@
 
             return carry
 
+        tail()
         lax.fori_loop(0, half + 1, finish, 0)
-        wait(buf.at[pl.ds(0, (nz * NX - 1) * m)], send)
 
     load_basis.wait()
 
@@ -280,7 +283,7 @@
 
         lax.fori_loop(0, nblk // 2, body, 0)
 
-    gather(vbuf, 2 * nb, v_send.at[0], v_z, v_l, v_r, v_o, v_a, make_blend, lambda j: None)
+    gather(vbuf, 2 * nb, v_send.at[0], v_z, v_l, v_r, v_o, v_a, make_blend, lambda j: None, lambda: None)
 
     def project(c, acc):
         cut = pl.ds(pl.multiple_of(c * 256, 256), 256)
@@ -316,22 +319,25 @@
 
         lax.fori_loop(1, nt, send_sum, 0)
         wait(proj.at[pl.ds(0, (nt - 1) * share)], s_recv.at[1])
-        wait(rsbuf, s_send.at[0])
-        wait(proj.at[pl.ds(0, (nt - 1) * share)], s_send.at[1])
     else:
         proj[...] = part[...]
 
     full = proj[...]
-    gram[...] = dot_full(full, full, TN)
     gshare = RANK // nt
     ng = 2 * gshare // 4
     mg = ng // nz
-    mine = gram[pl.ds(t * gshare, gshare), :]
-    for r in range(gshare // 4):
-        for c in range(2):
-            gslice[2 * r + c] = mine[4 * r : 4 * r + 4, 128 * c : 128 * c + 128]
+
+    def make_gram():
+        square = proj[...]
+        gram[...] = dot_full(square, square, TN)
+        mine = gram[pl.ds(t * gshare, gshare), :]
+        for r in range(gshare // 4):
+            for c in range(2):
+                gslice[2 * r + c] = mine[4 * r : 4 * r + 4, 128 * c : 128 * c + 128]
 
     def gram_send():
+        make_gram()
+
         def body(r, carry):
             peer = zmod(z + r)
             remote(
@@ -378,10 +384,6 @@
     def gram_done():
         if nt > 1:
             wait(gall.at[pl.ds(0, (nt - 1) * ng)], s_recv.at[5])
-            wait(gall.at[pl.ds(0, (nt - 1) * ng)], s_send.at[5])
-        wait(grs, s_send.at[2])
-        wait(gx.at[pl.ds(0, NX - 1)], s_send.at[3])
-        wait(gall.at[pl.ds(0, (nz - 1) * mg)], s_send.at[4])
         for r in range(RANK // 8):
             for c in range(2):
                 pair = [gall[4 * r + c], gall[4 * r + 2 + c]]
@@ -390,8 +392,6 @@
         across = lax.broadcasted_iota(jnp.int32, (RANK, RANK), 1)
         elim[:, RANK:] = jnp.where(down == across, 1.0, 0.0).astype(F32)
 
-    gram_send()
-
     turned = split(full.T)
     for h, start, width in cuts_of(nh):
         cut = slice((h * nh + start) * 128, (h * nh + start + width) * 128)
@@ -419,11 +419,12 @@
         ref[...] = ref[...] + other[...]
 
     def stage_a(q, s):
-        remote(wat(q, opp), piece(ropp, q), r_send.at[0], r_o.at[q], (to_right, to_left)[s]).start()
+        remote(wat(q, opp), piece(ropp, q), r_send.at[0], r_o.at[q], (to_right, to_left, to_opp)[s]).start()
 
     def stage_b(q, s):
-        wait(piece(ropp, q), r_o.at[q])
-        add_into(wat(q, (right, left)[s]), piece(ropp, q))
+        if s < 2:
+            wait(piece(ropp, q), r_o.at[q])
+            add_into(wat(q, (right, left)[s]), piece(ropp, q))
         remote(wat(q, right), piece(rleft, q), r_send.at[0], r_l.at[q], to_right).start()
         remote(wat(q, left), piece(rright, q), r_send.at[0], r_r.at[q], to_left).start()
 
@@ -486,6 +487,12 @@
         args = (piece, rodd, reven, r_odd, r_even)
         q = zmod(z - j)
         stage_c(q)
+
+        @pl.when(j == half)
+        def _():
+            wait(piece(ropp, q), r_o.at[q])
+            add_into(wat(q, x), piece(ropp, q))
+
         z_sum(j, half, q, wat(q, x), *args, to_down, to_down2, False)
 
         @pl.when((j >= 1) & (j < half))
@@ -531,32 +538,39 @@
         elim[here, :] = done
 
     def reduce_step(i, carry):
-        @pl.when(i <= half)
+        @pl.when(i == 0)
+        def _():
+            q = zmod(z - half)
+            stage_a(q, 2)
+            stage_b(q, 2)
+
+        @pl.when((i >= 1) & (i < half))
         def _():
             stage_a(zmod(z - half + i), 0)
 
-        @pl.when((i >= 1) & (i < half))
+        @pl.when((i >= 1) & (i <= half))
         def _():
             stage_a(zmod(z + half - i), 1)
 
+        @pl.when(i >= LAG_C)
+        def _():
+            late_sum(half + LAG_C - i)
+
+        @pl.when((i >= LAG_S) & (i <= half + LAG_S))
+        def _():
+            early_sum(half + LAG_S - i)
+
         b = i - LAG_B
 
-        @pl.when((b >= 0) & (b <= half))
+        @pl.when((b >= 1) & (b < half))
         def _():
             stage_b(zmod(z - half + b), 0)
 
-        @pl.when((b >= 1) & (b < half))
+        @pl.when((b >= 1) & (b <= half))
         def _():
             stage_b(zmod(z + half - b), 1)
 
-        @pl.when((i >= LAG_S) & (i <= half + LAG_S))
-        def _():
-            early_sum(half + LAG_S - i)
-
-        @pl.when(i >= LAG_C)
-        def _():
-            late_sum(half + LAG_C - i)
-
+        pl.when(i == 0)(gram_send)
         last = half + LAG_C
         for place, work in zip(GRAM_AT, (gram_over_z, gram_over_x, gram_over_t, gram_done)):
             pl.when(i == min(place, last))(work)
@@ -572,6 +586,11 @@
     wfin[pl.ds(f * m, m), 0:nb] = wat(z, x)[...]
     wfin[pl.ds(f * m, m), nb:] = jnp.sum(across[...].reshape(NX, m, na, 8, 128), axis=0)
 
+    def make_ortho():
+        inv_lower = elim[:, RANK:]
+        ortho_f32[...] = dot_full(proj[...], inv_lower, NT)
+        lhi[...], llo[...] = split(inv_lower)
+
     begun = max(0, half + LAG_C - max(GRAM_AT))
 
     def panels(j):
@@ -583,12 +602,9 @@
                 b = begun + (lax.div(j, 2) - (1 if half > 1 else 0)) * per + k
                 pl.when(b < npanel)(functools.partial(panel, b))
 
-    gather(wfin, nb, w_send.at[0], w_z, w_l, w_r, w_o, w_a, lambda: None, panels)
-    wait(wbuf.at[pl.ds(0, (nz * NX - 1) * m)], r_send.at[0])
-
-    inv_lower = elim[:, RANK:]
-    ortho = dot_full(proj[...], inv_lower, NT)
-    low = split(inv_lower)
+    gather(wfin, nb, w_send.at[0], w_z, w_l, w_r, w_o, w_a, lambda: None, panels, make_ortho)
+
+    low = lhi[...], llo[...]
     squared = jnp.zeros((RANK, 128), F32)
     stores = []
     for n, (h, start, width) in enumerate(cuts_of(nh)):
@@ -616,10 +632,10 @@
 
         lax.fori_loop(1, nt, send_norm, 0)
 
+    ortho = ortho_f32[...]
     ortho_out[...] = ortho.astype(BF16)
     if nt > 1:
         wait(nbuf.at[pl.ds(0, nt - 1)], s_recv.at[6])
-        wait(nbuf.at[pl.ds(0, nt - 1)], s_send.at[6])
     norm = nbuf[0]
     for r in range(1, nt):
         norm = norm + nbuf[r]
@@ -627,6 +643,16 @@
     scaled_high[...], scaled_low[...] = split(ortho * (inverse[0:1, :] * -factor))
     for store in stores:
         store.wait()
+    for buf, sem in ((vbuf, v_send), (wbuf, r_send), (wfin, w_send)):
+        wait(buf.at[pl.ds(0, (nz * NX - 1) * m)], sem.at[0])
+    if nt > 1:
+        wait(rsbuf, s_send.at[0])
+        wait(proj.at[pl.ds(0, (nt - 1) * share)], s_send.at[1])
+        wait(gall.at[pl.ds(0, (nt - 1) * ng)], s_send.at[5])
+        wait(nbuf.at[pl.ds(0, nt - 1)], s_send.at[6])
+    wait(grs, s_send.at[2])
+    wait(gx.at[pl.ds(0, NX - 1)], s_send.at[3])
+    wait(gall.at[pl.ds(0, (nz - 1) * mg)], s_send.at[4])
 
 
 def update(
@@ -716,6 +742,9 @@
             vmem((RANK, cols), BF16),
             vmem((RANK, cols), BF16),
             vmem((nt, 8, RANK), F32),
+            vmem((rows, RANK), F32),
+            vmem((RANK, RANK), BF16),
+            vmem((RANK, RANK), BF16),
             dma((3,)),
             dma((2 * ncut,)),
             dma((1,)), dma((nz,)), dma((nz,)), dma((nz,)), dma((nz,)), dma((nz + 1,)),

time: 141 us -> 140 us (level)
  no operation moved by 1% of the time
where the time goes in v5:
time: 140 us
  Pallas kernels  139 us (99%)
    pallas_call x1, Pallas kernels, per_device(): pl.pallas_call(functools.partial(kernel, nz, nt, factor), out_shape=(jax....  134 us
    pallas_call x1, Pallas kernels, per_device(): pl.pallas_call(update, out_shape=(jax.ShapeDtypeStruct((rows, cols), F32)...  5.34 us

profile of v5, /device:TPU:1, one launch (start us, length us, event | category | flops | bytes accessed | tf_op | source)
XLA Modules:
  0.0 139.9 jit_solution(14904479215393690758)
XLA Ops:
  0.6 133.9 %dion_step.1 = (bf16[256,3328]{1,0:T(8,128)(2,1)}, bf16[256,3328]{1,0:T(8,128)(2,1)}, bf16[128,256]{1,0:T(8,128)(2,1)}, bf16[128,256]{1,0:T(8,128)(2,1)}, bf16[128,256]{1,0:T(8,128)(2,1)}) custom-call(f32[128,3328]{1,0:T(8,128)} %mom_hbm.3, bf16[128,3328]{1,0:T(8,128)(2,1)} %grad_hbm.3, f32[1,26,4,128]{3,2,1,0:T(4,128)} %bitcast.3), custom_call_target="tpu_custom_call" | custom-call | tf_op jit(solution)/shard_map/dion_step/pallas_call | solution.py:705
  134.6 5.3 %dion_update.1 = (f32[128,3328]{1,0:T(8,128)}, bf16[128,3328]{1,0:T(8,128)(2,1)}) custom-call(f32[128,3328]{1,0:T(8,128)} %mom_hbm.3, bf16[128,3328]{1,0:T(8,128)(2,1)} %grad_hbm.3, bf16[256,3328]{1,0:T(8,128)(2,1)} %get-tuple-element.7.high_hbm, bf16[256,3328]{1,0:T(8,128)(2,1)} %get-tuple-element.8.low_hbm, bf16[128,256]{1,0:T(8,128)(2,1)} %get-tuple-element.9.ortho, ...), custom_call_target="tpu_custom_call" | custom-call | tf_op jit(solution)/shard_map/dion_update/pallas_call | solution.py:762

commit v6 on v5

--- a/solution.py
+++ b/solution.py
@@ -98,6 +98,12 @@
     def dev(zz, xx):
         return (zz * NX + xx, t)
 
+    def far_t(r):
+        return lax.rem(r + max(nt // 4 - 1, 0), max(nt - 1, 1)) + 1
+
+    def far_z(r):
+        return lax.rem(r + half - 2, nz - 1) + 1
+
     to_up, to_down = dev(zmod(z + 1), x), dev(zmod(z - 1), x)
     to_up2, to_down2 = dev(zmod(z + 2), x), dev(zmod(z - 2 + nz), x)
     to_left, to_right, to_opp = dev(z, left), dev(z, right), dev(z, opp)
@@ -297,6 +303,7 @@
         own = pl.ds(t * share, share)
 
         def send_part(r, carry):
+            r = far_t(r)
             peer = tmod(t + r)
             remote(
                 part.at[pl.ds(peer * share, share)], rsbuf.at[r - 1],
@@ -313,7 +320,7 @@
 
         def send_sum(r, carry):
             remote(
-                proj.at[own], proj.at[own], s_send.at[1], s_recv.at[1], (f, tmod(t + r))
+                proj.at[own], proj.at[own], s_send.at[1], s_recv.at[1], (f, tmod(t + far_t(r)))
             ).start()
             return carry
 
@@ -339,6 +346,7 @@
         make_gram()
 
         def body(r, carry):
+            r = far_z(r)
             peer = zmod(z + r)
             remote(
                 gslice.at[pl.ds(peer * mg, mg)], grs.at[r - 1],
@@ -362,7 +370,7 @@
 
         def body(r, carry):
             remote(
-                gall.at[here], gall.at[here], s_send.at[4], s_recv.at[4], dev(zmod(z + r), x)
+                gall.at[here], gall.at[here], s_send.at[4], s_recv.at[4], dev(zmod(z + far_z(r)), x)
             ).start()
             return carry
 
@@ -375,7 +383,7 @@
 
             def body(r, carry):
                 remote(
-                    gall.at[here], gall.at[here], s_send.at[5], s_recv.at[5], (f, tmod(t + r))
+                    gall.at[here], gall.at[here], s_send.at[5], s_recv.at[5], (f, tmod(t + far_t(r)))
                 ).start()
                 return carry
 
@@ -626,7 +634,7 @@
     if nt > 1:
         def send_norm(r, carry):
             remote(
-                nbuf.at[t], nbuf.at[t], s_send.at[6], s_recv.at[6], (f, tmod(t + r))
+                nbuf.at[t], nbuf.at[t], s_send.at[6], s_recv.at[6], (f, tmod(t + far_t(r)))
             ).start()
             return carry
 

time: 140 us -> 139 us (level)
  no operation moved by 1% of the time
where the time goes in v6:
time: 139 us
  Pallas kernels  138 us (99%)
    pallas_call x1, Pallas kernels, per_device(): pl.pallas_call(functools.partial(kernel, nz, nt, factor), out_shape=(jax....  133 us
    pallas_call x1, Pallas kernels, per_device(): pl.pallas_call(update, out_shape=(jax.ShapeDtypeStruct((rows, cols), F32)...  5.34 us

profile of v6, /device:TPU:1, one launch (start us, length us, event | category | flops | bytes accessed | tf_op | source)
XLA Modules:
  0.0 138.7 jit_solution(6692044322809087810)
XLA Ops:
  0.6 132.7 %dion_step.1 = (bf16[256,3328]{1,0:T(8,128)(2,1)}, bf16[256,3328]{1,0:T(8,128)(2,1)}, bf16[128,256]{1,0:T(8,128)(2,1)}, bf16[128,256]{1,0:T(8,128)(2,1)}, bf16[128,256]{1,0:T(8,128)(2,1)}) custom-call(f32[128,3328]{1,0:T(8,128)} %mom_hbm.3, bf16[128,3328]{1,0:T(8,128)(2,1)} %grad_hbm.3, f32[1,26,4,128]{3,2,1,0:T(4,128)} %bitcast.3), custom_call_target="tpu_custom_call" | custom-call | tf_op jit(solution)/shard_map/dion_step/pallas_call | solution.py:713
  133.4 5.3 %dion_update.1 = (f32[128,3328]{1,0:T(8,128)}, bf16[128,3328]{1,0:T(8,128)(2,1)}) custom-call(f32[128,3328]{1,0:T(8,128)} %mom_hbm.3, bf16[128,3328]{1,0:T(8,128)(2,1)} %grad_hbm.3, bf16[256,3328]{1,0:T(8,128)(2,1)} %get-tuple-element.7.high_hbm, bf16[256,3328]{1,0:T(8,128)(2,1)} %get-tuple-element.8.low_hbm, bf16[128,256]{1,0:T(8,128)(2,1)} %get-tuple-element.9.ortho, ...), custom_call_target="tpu_custom_call" | custom-call | tf_op jit(solution)/shard_map/dion_update/pallas_call | solution.py:770
